TPU v7x, 32 devices: a whole 2x2x4 slice. The times are simulated.
32 devices in a mesh: orbit: 8 (over z, core), space: 4 (over y, x).
Axes of the slice: x: 2, y: 2, z: 4, core: 2. Of those that a mesh axis runs over, the one named last changes fastest.
Arguments:
- queries: bfloat16 [8, 8, 64, 2240], P('orbit', 'space'), may hold values from -6 to 6
- keys_in: bfloat16 [8, 8, 64, 2240], P('orbit', 'space'), may hold values from -6 to 6
- values: bfloat16 [8, 8, 64, 2240], P('orbit', 'space'), may hold values from -6 to 6
- conv_weight: bfloat16 [3, 3, 2240], replicated, may hold values from -2 to 2
- grad_out: bfloat16 [8, 8, 64, 2240], P('orbit', 'space'), may hold values from -6 to 6
Outputs:
- attended: bfloat16 [8, 8, 64, 2240], P('orbit', 'space')
- grad_query: bfloat16 [8, 8, 64, 2240], P('orbit', 'space')
- grad_key: bfloat16 [8, 8, 64, 2240], P('orbit', 'space')
- grad_value: bfloat16 [8, 8, 64, 2240], P('orbit', 'space')
All inputs are finite; a program needn't handle non-finite values.
Results may differ from a plain program's by a relative error of at most 0.0079.
Values may be sent and summed in bfloat16 or wider, within the bound.
A program may use at most 128 MiB of HBM per device.

v0:
```python
import functools
import math

import jax
import jax.numpy as jnp
from jax import lax
from jax.experimental import pallas as pl
from jax.experimental.pallas import tpu as pltpu
from jax.sharding import PartitionSpec as P

HEADS = 20
HD = 112
LANES = 128
GROUP = 4
GROUPS = HEADS // GROUP
BF = jnp.bfloat16
F32 = jnp.float32
MESH = pl.DeviceIdType.MESH


def dot_tn(a, b):
    return lax.dot_general(a, b, (((0,), (0,)), ((), ())), preferred_element_type=F32)


def dot_nt(a, b):
    return lax.dot_general(a, b, (((1,), (1,)), ((), ())), preferred_element_type=F32)


def dot_nn(a, b):
    return lax.dot_general(a, b, (((1,), (0,)), ((), ())), preferred_element_type=F32)


def kernel(
    nz, n1, n2, chunk,
    q_ref, k_ref, v_ref, w_ref, g_ref,
    att_ref, gq_ref, gk_ref, gv_ref,
    vx, kx, gx, att32, gq32, gk32, gv32, halo_v, halo_g,
    st32, st16, a32, a16, p32, t16, rs1, rs2, pc, zr, full,
    halo_ss, halo_rs, rs1_ss, rs1_rs, rs2_ss, rs2_rs, pc_ss, pc_rs, zr_ss, zr_rs,
    agx_ss, agx_rs, agy_ss, agy_rs,
):
    rows, cols, width = v_ref.shape
    tokens = rows * cols
    n = n1 * n2
    wide = n2 * chunk
    group_rows = GROUP * HD
    u = lax.axis_index("orbit")
    s = lax.axis_index("space")
    z, core = u // 2, u % 2
    y, x = s // n2, s % n2
    count = (u + 1).astype(F32) * float(rows * n * cols)
    inv_count = 1.0 / count
    pair = z * 2 + (1 - core)

    def y_peer(k):
        return {"space": lax.rem(y + k, n1) * n2 + x}

    def x_peer(k):
        return {"space": y * n2 + lax.rem(x + k, n2)}

    def z_peer(k):
        return {"orbit": (z + k) * 2 + core}

    barrier = pltpu.get_barrier_semaphore()
    for k in range(1, n1):
        pl.semaphore_signal(barrier, inc=1, device_id=y_peer(k), device_id_type=MESH)
    for k in range(1, n2):
        pl.semaphore_signal(barrier, inc=1, device_id=x_peer(k), device_id_type=MESH)
    pl.semaphore_signal(barrier, inc=1, device_id={"orbit": pair}, device_id_type=MESH)
    for k in range(1, nz):
        pl.semaphore_signal(
            barrier, inc=1, device_id={"orbit": lax.rem(z + k, nz) * 2 + core},
            device_id_type=MESH,
        )

    @pl.when(s > 0)
    def _():
        pl.semaphore_signal(barrier, inc=1, device_id={"space": s - 1}, device_id_type=MESH)

    @pl.when(s < n - 1)
    def _():
        pl.semaphore_signal(barrier, inc=1, device_id={"space": s + 1}, device_id_type=MESH)

    lane = lax.broadcasted_iota(jnp.int32, (tokens, LANES), 1)
    ones_column = jnp.where(lane == HD, 1.0, 0.0).astype(BF)
    zero_block = jnp.zeros((tokens, LANES), BF)

    def columns(h):
        return slice(h * HD, (h + 1) * HD)

    def flat(ref, where):
        return ref[:, :, where].reshape(tokens, -1)

    def put_state(ph, g, j, block):
        st32[ph, g, j * HD:(j + 1) * HD] = block
        st16[ph, g, j * HD:(j + 1) * HD] = block.astype(BF)

    def pad_state(ph, g):
        if n * chunk > group_rows:
            extra = n * chunk - group_rows
            st32[ph, g, group_rows:] = jnp.zeros((extra, LANES), F32)
            st16[ph, g, group_rows:] = jnp.zeros((extra, LANES), BF)

    def remote(src, dst, ss, rs, to):
        return pltpu.make_async_remote_copy(
            src_ref=src, dst_ref=dst, send_sem=ss, recv_sem=rs,
            device_id=to, device_id_type=MESH,
        )

    def copy_rs1(ph, g, k):
        part = st16.at[ph, g, pl.ds(lax.rem(y + k, n1) * wide, wide)]
        i = (ph, g, k - 1)
        return remote(part, rs1.at[i], rs1_ss.at[i], rs1_rs.at[i], y_peer(k))

    def copy_rs2(ph, g, k):
        part = a16.at[ph, g, pl.ds(lax.rem(x + k, n2) * chunk, chunk)]
        i = (ph, g, k - 1)
        return remote(part, rs2.at[i], rs2_ss.at[i], rs2_rs.at[i], x_peer(k))

    def copy_pc(ph, g):
        i = (ph, g)
        return remote(p32.at[i], pc.at[i], pc_ss.at[i], pc_rs.at[i], {"orbit": pair})

    def copy_zr(ph, g, k):
        i = (ph, g, k - 1)
        return remote(
            t16.at[ph, g], zr.at[i], zr_ss.at[i], zr_rs.at[i], z_peer(k if ph == 0 else -k)
        )

    def z_sends(ph, k):
        return (z + k < nz) if ph == 0 else (z - k >= 0)

    def z_gets(ph, k):
        return (z - k >= 0) if ph == 0 else (z + k < nz)

    def copy_agx(ph, g, k):
        i = (ph, g, k - 1)
        here = full.at[ph, g, pl.ds(s * chunk, chunk)]
        return remote(here, here, agx_ss.at[i], agx_rs.at[i], x_peer(k))

    def got_agx(ph, g, k):
        i = (ph, g, k - 1)
        there = full.at[ph, g, pl.ds((y * n2 + lax.rem(x + n2 - k, n2)) * chunk, chunk)]
        return remote(there, there, agx_ss.at[i], agx_rs.at[i], x_peer(k))

    def copy_agy(ph, g, k):
        i = (ph, g, k - 1)
        here = full.at[ph, g, pl.ds(y * wide, wide)]
        return remote(here, here, agy_ss.at[i], agy_rs.at[i], y_peer(k))

    def got_agy(ph, g, k):
        i = (ph, g, k - 1)
        there = full.at[ph, g, pl.ds(lax.rem(y + n1 - k, n1) * wide, wide)]
        return remote(there, there, agy_ss.at[i], agy_rs.at[i], y_peer(k))

    def halo_down(src, halo, i):
        return remote(
            src.at[rows - 1], halo.at[0], halo_ss.at[i], halo_rs.at[i], {"space": s + 1}
        )

    def halo_up(src, halo, i):
        return remote(src.at[0], halo.at[1], halo_ss.at[i], halo_rs.at[i], {"space": s - 1})

    def start_halo(src, halo, i):
        @pl.when(s < n - 1)
        def _():
            halo_down(src, halo, i).start()

        @pl.when(s > 0)
        def _():
            halo_up(src, halo, i + 1).start()

    def wait_halo(src, halo, i):
        @pl.when(s > 0)
        def _():
            halo_down(src, halo, i).wait_recv()

        @pl.when(s == 0)
        def _():
            halo[0] = jnp.zeros((cols, width), BF)

        @pl.when(s < n - 1)
        def _():
            halo_up(src, halo, i + 1).wait_recv()

        @pl.when(s == n - 1)
        def _():
            halo[1] = jnp.zeros((cols, width), BF)

    def drain_halo(src, halo, i):
        @pl.when(s < n - 1)
        def _():
            halo_down(src, halo, i).wait_send()

        @pl.when(s > 0)
        def _():
            halo_up(src, halo, i + 1).wait_send()

    def keys_step(g):
        for j in range(GROUP):
            h = g * GROUP + j
            kx[h] = jnp.maximum(flat(k_ref, columns(h)), 0)
            vx[h] = ones_column
            vx[h, :, :HD] = flat(v_ref, columns(h))
            put_state(0, g, j, dot_tn(kx[h], vx[h]))
        pad_state(0, g)

    def query_step(g):
        for j in range(GROUP):
            h = g * GROUP + j
            state = full[0, g, j * HD:(j + 1) * HD]
            query = jnp.maximum(flat(q_ref, columns(h)), 0)
            gx[h] = zero_block
            gx[h, :, :HD] = flat(g_ref, columns(h))
            grad = gx[h].astype(F32)
            numerator = dot_nn(query, state)
            inverse = 1.0 / (numerator[:, HD:HD + 1] + 1.0)
            den_grad = -jnp.sum(grad * numerator, axis=1, keepdims=True) * (inverse * inverse)
            num_grad = jnp.where(lane == HD, den_grad, grad * inverse).astype(BF)
            att32[:, columns(h)] = (numerator * inverse)[:, :HD]
            gq32[:, columns(h)] = dot_nt(num_grad, state)
            put_state(1, g, j, dot_tn(query, num_grad))
        pad_state(1, g)

    def last_step(g):
        for j in range(GROUP):
            h = g * GROUP + j
            state = full[1, g, j * HD:(j + 1) * HD]
            gk32[:, columns(h)] = dot_nt(vx[h], state)
            gv32[:, columns(h)] = dot_nn(kx[h], state)[:, :HD]

    def send_rs1(ph, g):
        for k in range(1, n1):
            copy_rs1(ph, g, k).start()

    def step_rs2(ph, g):
        total = st32[ph, g, pl.ds(y * wide, wide)]
        for k in range(1, n1):
            copy_rs1(ph, g, k).wait_recv()
            total = total + rs1[ph, g, k - 1].astype(F32)
        a32[ph, g] = total
        a16[ph, g] = total.astype(BF)
        for k in range(1, n2):
            copy_rs2(ph, g, k).start()

    def step_pc(ph, g):
        total = a32[ph, g, pl.ds(x * chunk, chunk)]
        for k in range(1, n2):
            copy_rs2(ph, g, k).wait_recv()
            total = total + rs2[ph, g, k - 1].astype(F32)
        if ph == 1:
            total = total * inv_count
        p32[ph, g] = total
        copy_pc(ph, g).start()

    def step_z(ph, g):
        copy_pc(ph, g).wait_recv()
        t16[ph, g] = (p32[ph, g] + pc[ph, g]).astype(BF)
        for k in range(1, nz):
            @pl.when(z_sends(ph, k))
            def _():
                copy_zr(ph, g, k).start()

    def step_agx(ph, g):
        with_pair = core if ph == 0 else 1 - core
        a32[ph, g, :chunk] = p32[ph, g] + pc[ph, g] * with_pair.astype(F32)
        for k in range(1, nz):
            @pl.when(z_gets(ph, k))
            def _():
                copy_zr(ph, g, k).wait_recv()
                a32[ph, g, :chunk] += zr[ph, g, k - 1].astype(F32)
        total = a32[ph, g, :chunk]
        if ph == 0:
            total = total * inv_count
        full[ph, g, pl.ds(s * chunk, chunk)] = total.astype(BF)
        for k in range(1, n2):
            copy_agx(ph, g, k).start()

    def step_agy(ph, g):
        for k in range(1, n2):
            got_agx(ph, g, k).wait_recv()
        for k in range(1, n1):
            copy_agy(ph, g, k).start()

    def step_full(ph, g):
        for k in range(1, n1):
            got_agy(ph, g, k).wait_recv()

    def chain(step, g):
        if step == 0:
            keys_step(g)
            send_rs1(0, g)
        elif step == 6:
            step_full(0, g)
            query_step(g)
            send_rs1(1, g)
        elif step == 12:
            step_full(1, g)
            last_step(g)
        else:
            ph = 0 if step < 6 else 1
            (step_rs2, step_pc, step_z, step_agx, step_agy)[(step - 1) % 6](ph, g)

    col = lax.broadcasted_iota(jnp.int32, (tokens, 1), 0) % cols

    def filtered(src, halo, where, back):
        above = halo[0:1, :, where].astype(F32)
        here = src[:, :, where].astype(F32)
        below = halo[1:2, :, where].astype(F32)
        stack = jnp.concatenate([above, here, below], axis=0)
        sums = [None] * 3
        for a in range(3):
            weights = w_ref[a, :, where].astype(F32)
            first = 2 - a if back else a
            block = stack[first:first + rows].reshape(tokens, -1)
            for b in range(3):
                term = weights[b:b + 1] * block
                sums[b] = term if sums[b] is None else sums[b] + term
        left, right = (sums[2], sums[0]) if back else (sums[0], sums[2])
        left = jnp.where(col == 0, 0.0, pltpu.roll(left, 1, 0))
        right = jnp.where(col == cols - 1, 0.0, pltpu.roll(right, tokens - 1, 0))
        return sums[1] + left + right

    def over_lanes(body):
        whole = width // LANES

        @pl.loop(0, whole)
        def _(i):
            body(pl.ds(pl.multiple_of(i * LANES, LANES), LANES), LANES)

        if width % LANES:
            body(slice(whole * LANES, width), width % LANES)

    def shaped(block, size):
        return block.reshape(rows, cols, size)

    def finish_forward(where, size):
        block = att32[:, where] + filtered(v_ref, halo_v, where, False)
        att_ref[:, :, where] = shaped(block.astype(BF), size)
        queries = flat(q_ref, where).astype(F32)
        grads = jnp.where(queries > 0, gq32[:, where], 0.0)
        gq_ref[:, :, where] = shaped(grads.astype(BF), size)

    def conv_grads(where, size):
        att32[:, where] = filtered(g_ref, halo_g, where, True)

    def finish_backward(where, size):
        keys = flat(k_ref, where).astype(F32)
        grads = jnp.where(keys > 0, gk32[:, where], 0.0)
        gk_ref[:, :, where] = shaped(grads.astype(BF), size)
        gv_ref[:, :, where] = shaped((gv32[:, where] + att32[:, where]).astype(BF), size)

    fan = (n1 - 1) + (n2 - 1) + 1 + (nz - 1)
    pl.semaphore_wait(
        barrier, fan + jnp.where(s > 0, 1, 0) + jnp.where(s < n - 1, 1, 0)
    )

    start_halo(v_ref, halo_v, 0)
    for tick in range(12 + GROUPS):
        for g in range(GROUPS):
            step = tick - g
            if 0 <= step <= 12:
                chain(step, g)
        if tick == 4:
            start_halo(g_ref, halo_g, 2)
        if tick == 5 + GROUPS:
            wait_halo(v_ref, halo_v, 0)
            over_lanes(finish_forward)
            wait_halo(g_ref, halo_g, 2)
            over_lanes(conv_grads)
    over_lanes(finish_backward)

    drain_halo(v_ref, halo_v, 0)
    drain_halo(g_ref, halo_g, 2)
    for ph in range(2):
        for g in range(GROUPS):
            for k in range(1, n1):
                copy_rs1(ph, g, k).wait_send()
                copy_agy(ph, g, k).wait_send()
            for k in range(1, n2):
                copy_rs2(ph, g, k).wait_send()
                copy_agx(ph, g, k).wait_send()
            copy_pc(ph, g).wait_send()
            for k in range(1, nz):
                @pl.when(z_sends(ph, k))
                def _():
                    copy_zr(ph, g, k).wait_send()


def factors(n):
    first = math.isqrt(n)
    while n % first:
        first -= 1
    return first, n // first


def on_device(nz, n1, n2, queries, keys_in, values, conv_weight, grad_out):
    _, rows, cols, width = queries.shape
    tokens = rows * cols
    n = n1 * n2
    chunk = -(-GROUP * HD // (16 * n)) * 16
    shape3 = (rows, cols, width)
    vmem = pl.BlockSpec(memory_space=pltpu.VMEM)

    def dma(*shape):
        return pltpu.SemaphoreType.DMA(tuple(max(1, e) for e in shape))

    def buf(shape, dtype):
        return pltpu.VMEM(tuple(max(1, e) for e in shape), dtype)

    lead = (2, GROUPS)
    sems = [dma(4), dma(4)]
    for tail in ((n1 - 1,), (n2 - 1,), (), (nz - 1,), (n2 - 1,), (n1 - 1,)):
        sems += [dma(*lead, *tail), dma(*lead, *tail)]
    outs = pl.pallas_call(
        functools.partial(kernel, nz, n1, n2, chunk),
        out_shape=[jax.ShapeDtypeStruct(shape3, BF)] * 4,
        in_specs=[vmem] * 5,
        out_specs=[vmem] * 4,
        scratch_shapes=[
            buf((HEADS, tokens, LANES), BF),
            buf((HEADS, tokens, HD), BF),
            buf((HEADS, tokens, LANES), BF),
            buf((tokens, width), F32),
            buf((tokens, width), F32),
            buf((tokens, width), F32),
            buf((tokens, width), F32),
            buf((2, cols, width), BF),
            buf((2, cols, width), BF),
            buf((*lead, n * chunk, LANES), F32),
            buf((*lead, n * chunk, LANES), BF),
            buf((*lead, n2 * chunk, LANES), F32),
            buf((*lead, n2 * chunk, LANES), BF),
            buf((*lead, chunk, LANES), F32),
            buf((*lead, chunk, LANES), BF),
            buf((*lead, n1 - 1, n2 * chunk, LANES), BF),
            buf((*lead, n2 - 1, chunk, LANES), BF),
            buf((*lead, chunk, LANES), F32),
            buf((*lead, nz - 1, chunk, LANES), BF),
            buf((*lead, n * chunk, LANES), BF),
            *sems,
        ],
        compiler_params=pltpu.CompilerParams(
            collective_id=0, has_side_effects=True, vmem_limit_bytes=48 * 2**20
        ),
    )(
        queries.reshape(shape3), keys_in.reshape(shape3), values.reshape(shape3),
        conv_weight, grad_out.reshape(shape3),
    )
    return tuple(o.reshape(queries.shape) for o in outs)


def solution(mesh):
    nz = mesh.shape["orbit"] // 2
    n1, n2 = factors(mesh.shape["space"])
    field = P("orbit", "space", None, None)
    return jax.shard_map(
        functools.partial(on_device, nz, n1, n2),
        mesh=mesh,
        in_specs=(field, field, field, P(), field),
        out_specs=(field, field, field, field),
        check_vma=False,
    )
```

profile of v0, /device:TPU:0, one launch (start us, length us, event | category | flops | bytes accessed | tf_op | source)
XLA Modules:
  0.0 95.2 jit_solution(14514155618394953364)
XLA Ops:
  0.6 0.0 copy-start
  0.6 1.1 %copy-done = bf16[1,2,64,2240]{3,2,1,0:T(8,128)(2,1)S(1)} copy-done((bf16[1,2,64,2240]{3,2,1,0:T(8,128)(2,1)S(1)}, bf16[1,2,64,2240]{3,2,1,0:T(8,128)(2,1)}, u32[]{:S(2)}) %copy-start) | copy-done | bytes 573464
  1.7 0.0 copy-start.1
  1.7 1.1 %copy-done.1 = bf16[1,2,64,2240]{3,2,1,0:T(8,128)(2,1)S(1)} copy-done((bf16[1,2,64,2240]{3,2,1,0:T(8,128)(2,1)S(1)}, bf16[1,2,64,2240]{3,2,1,0:T(8,128)(2,1)}, u32[]{:S(2)}) %copy-start.1) | copy-done | bytes 573464
  2.8 0.0 copy-start.2
  2.8 1.1 %copy-done.2 = bf16[1,2,64,2240]{3,2,1,0:T(8,128)(2,1)S(1)} copy-done((bf16[1,2,64,2240]{3,2,1,0:T(8,128)(2,1)S(1)}, bf16[1,2,64,2240]{3,2,1,0:T(8,128)(2,1)}, u32[]{:S(2)}) %copy-start.2) | copy-done | bytes 573464
  3.8 0.0 copy-start.3
  3.8 1.1 %copy-done.3 = bf16[1,2,64,2240]{3,2,1,0:T(8,128)(2,1)S(1)} copy-done((bf16[1,2,64,2240]{3,2,1,0:T(8,128)(2,1)S(1)}, bf16[1,2,64,2240]{3,2,1,0:T(8,128)(2,1)}, u32[]{:S(2)}) %copy-start.3) | copy-done | bytes 573464
  4.9 0.0 copy-start.4
  4.9 0.8 copy-done.4
  5.7 86.2 %shard_map.84 = (bf16[2,64,2240]{2,1,0:T(8,128)(2,1)S(1)}, bf16[2,64,2240]{2,1,0:T(8,128)(2,1)S(1)}, bf16[2,64,2240]{2,1,0:T(8,128)(2,1)S(1)}, bf16[2,64,2240]{2,1,0:T(8,128)(2,1)S(1)}) custom-call(bf16[2,64,2240]{2,1,0:T(8,128)(2,1)S(1)} %bitcast.12, bf16[2,64,2240]{2,1,0:T(8,128)(2,1)S(1)} %bitcast.13, bf16[2,64,2240]{2,1,0:T(8,128)(2,1)S(1)} %bitcast.14, ...), custom_call_target="tpu_custom_call" | custom-call | tf_op jit(solution)/shard_map/pallas_call | solution.py:415
  92.0 0.8 copy.13
  92.8 0.8 copy.14
  93.6 0.8 copy.15
  94.4 0.8 copy.16
Async XLA Ops:
  0.6 1.1 %copy-start = (bf16[1,2,64,2240]{3,2,1,0:T(8,128)(2,1)S(1)}, bf16[1,2,64,2240]{3,2,1,0:T(8,128)(2,1)}, u32[]{:S(2)}) copy-start(bf16[1,2,64,2240]{3,2,1,0:T(8,128)(2,1)} %param.5) | copy-start | bytes 1720324
  1.7 1.1 %copy-start.1 = (bf16[1,2,64,2240]{3,2,1,0:T(8,128)(2,1)S(1)}, bf16[1,2,64,2240]{3,2,1,0:T(8,128)(2,1)}, u32[]{:S(2)}) copy-start(bf16[1,2,64,2240]{3,2,1,0:T(8,128)(2,1)} %param.6) | copy-start | bytes 1720324
  2.8 1.1 %copy-start.2 = (bf16[1,2,64,2240]{3,2,1,0:T(8,128)(2,1)S(1)}, bf16[1,2,64,2240]{3,2,1,0:T(8,128)(2,1)}, u32[]{:S(2)}) copy-start(bf16[1,2,64,2240]{3,2,1,0:T(8,128)(2,1)} %param.7) | copy-start | bytes 1720324
  3.8 1.1 %copy-start.3 = (bf16[1,2,64,2240]{3,2,1,0:T(8,128)(2,1)S(1)}, bf16[1,2,64,2240]{3,2,1,0:T(8,128)(2,1)}, u32[]{:S(2)}) copy-start(bf16[1,2,64,2240]{3,2,1,0:T(8,128)(2,1)} %param.9) | copy-start | bytes 1720324
  4.9 0.8 copy-start.4
where the time goes:
time: 95.6 us; the launch traced here: 95.2 us
  Pallas kernels  86.2 us (90%)
  local copies, waits for them, and re-layouts  8.32 us (9%)
    pallas_call x1, Pallas kernels, on_device(): pl.pallas_call(functools.partial(kernel, nz, n1, n2, chunk), out_shape=[j...  86.2 us
    unnamed x14, local copies, waits for them, and re-layouts  8.32 us

commit v1 on v0

--- a/solution.py
+++ b/solution.py
@@ -13,6 +13,12 @@
 LANES = 128
 GROUP = 4
 GROUPS = HEADS // GROUP
+PIECE = 16
+VALUE_HALO = 0
+GRAD_HALO = 5
+QUERY_TICK = 6
+FORWARD_TICK = 8
+CONV_TICK = 11
 BF = jnp.bfloat16
 F32 = jnp.float32
 MESH = pl.DeviceIdType.MESH
@@ -32,9 +38,10 @@
 
 def kernel(
     nz, n1, n2, chunk,
-    q_ref, k_ref, v_ref, w_ref, g_ref,
+    q_hbm, k_hbm, v_hbm, w_hbm, g_hbm,
     att_ref, gq_ref, gk_ref, gv_ref,
-    vx, kx, gx, att32, gq32, gk32, gv32, halo_v, halo_g,
+    q_ref, k_ref, v_ref, w_ref, g_ref, in_sems,
+    vx, kx, gx, att32, gq32, gk32, gv32, conv32, halo_v, halo_g,
     st32, st16, a32, a16, p32, t16, rs1, rs2, pc, zr, full,
     halo_ss, halo_rs, rs1_ss, rs1_rs, rs2_ss, rs2_rs, pc_ss, pc_rs, zr_ss, zr_rs,
     agx_ss, agx_rs, agy_ss, agy_rs,
@@ -81,6 +88,15 @@
     def _():
         pl.semaphore_signal(barrier, inc=1, device_id={"space": s + 1}, device_id_type=MESH)
 
+    loads = [
+        pltpu.make_async_copy(src, dst, in_sems.at[i])
+        for i, (src, dst) in enumerate(
+            ((k_hbm, k_ref), (v_hbm, v_ref), (g_hbm, g_ref), (q_hbm, q_ref), (w_hbm, w_ref))
+        )
+    ]
+    for load in loads:
+        load.start()
+
     lane = lax.broadcasted_iota(jnp.int32, (tokens, LANES), 1)
     ones_column = jnp.where(lane == HD, 1.0, 0.0).astype(BF)
     zero_block = jnp.zeros((tokens, LANES), BF)
@@ -153,27 +169,36 @@
         there = full.at[ph, g, pl.ds(lax.rem(y + n1 - k, n1) * wide, wide)]
         return remote(there, there, agy_ss.at[i], agy_rs.at[i], y_peer(k))
 
-    def halo_down(src, halo, i):
+    pieces = cols // PIECE
+
+    def halo_down(src, halo, i, p):
+        part = pl.ds(p * PIECE, PIECE)
         return remote(
-            src.at[rows - 1], halo.at[0], halo_ss.at[i], halo_rs.at[i], {"space": s + 1}
+            src.at[rows - 1, part], halo.at[0, part], halo_ss.at[i, p], halo_rs.at[i, p],
+            {"space": s + 1},
         )
 
-    def halo_up(src, halo, i):
-        return remote(src.at[0], halo.at[1], halo_ss.at[i], halo_rs.at[i], {"space": s - 1})
-
-    def start_halo(src, halo, i):
+    def halo_up(src, halo, i, p):
+        part = pl.ds(p * PIECE, PIECE)
+        return remote(
+            src.at[0, part], halo.at[1, part], halo_ss.at[i + 1, p], halo_rs.at[i + 1, p],
+            {"space": s - 1},
+        )
+
+    def start_halo(src, halo, i, p):
         @pl.when(s < n - 1)
         def _():
-            halo_down(src, halo, i).start()
+            halo_down(src, halo, i, p).start()
 
         @pl.when(s > 0)
         def _():
-            halo_up(src, halo, i + 1).start()
+            halo_up(src, halo, i, p).start()
 
     def wait_halo(src, halo, i):
         @pl.when(s > 0)
         def _():
-            halo_down(src, halo, i).wait_recv()
+            for p in range(pieces):
+                halo_down(src, halo, i, p).wait_recv()
 
         @pl.when(s == 0)
         def _():
@@ -181,7 +206,8 @@
 
         @pl.when(s < n - 1)
         def _():
-            halo_up(src, halo, i + 1).wait_recv()
+            for p in range(pieces):
+                halo_up(src, halo, i, p).wait_recv()
 
         @pl.when(s == n - 1)
         def _():
@@ -190,11 +216,13 @@
     def drain_halo(src, halo, i):
         @pl.when(s < n - 1)
         def _():
-            halo_down(src, halo, i).wait_send()
+            for p in range(pieces):
+                halo_down(src, halo, i, p).wait_send()
 
         @pl.when(s > 0)
         def _():
-            halo_up(src, halo, i + 1).wait_send()
+            for p in range(pieces):
+                halo_up(src, halo, i, p).wait_send()
 
     def keys_step(g):
         for j in range(GROUP):
@@ -288,7 +316,8 @@
 
     def chain(step, g):
         if step == 0:
-            keys_step(g)
+            if g:
+                keys_step(g)
             send_rs1(0, g)
         elif step == 6:
             step_full(0, g)
@@ -321,15 +350,16 @@
         right = jnp.where(col == cols - 1, 0.0, pltpu.roll(right, tokens - 1, 0))
         return sums[1] + left + right
 
-    def over_lanes(body):
-        whole = width // LANES
-
-        @pl.loop(0, whole)
+    def over_lanes(body, g):
+        first = g * group_rows // LANES
+        last = (g + 1) * group_rows // LANES
+
+        @pl.loop(first, last)
         def _(i):
             body(pl.ds(pl.multiple_of(i * LANES, LANES), LANES), LANES)
 
-        if width % LANES:
-            body(slice(whole * LANES, width), width % LANES)
+        if g == GROUPS - 1 and width % LANES:
+            body(slice(last * LANES, width), width % LANES)
 
     def shaped(block, size):
         return block.reshape(rows, cols, size)
@@ -342,33 +372,50 @@
         gq_ref[:, :, where] = shaped(grads.astype(BF), size)
 
     def conv_grads(where, size):
-        att32[:, where] = filtered(g_ref, halo_g, where, True)
+        conv32[:, where] = filtered(g_ref, halo_g, where, True)
 
     def finish_backward(where, size):
         keys = flat(k_ref, where).astype(F32)
         grads = jnp.where(keys > 0, gk32[:, where], 0.0)
         gk_ref[:, :, where] = shaped(grads.astype(BF), size)
-        gv_ref[:, :, where] = shaped((gv32[:, where] + att32[:, where]).astype(BF), size)
-
+        gv_ref[:, :, where] = shaped((gv32[:, where] + conv32[:, where]).astype(BF), size)
+
+    for load in loads[:2]:
+        load.wait()
+    keys_step(0)
     fan = (n1 - 1) + (n2 - 1) + 1 + (nz - 1)
     pl.semaphore_wait(
         barrier, fan + jnp.where(s > 0, 1, 0) + jnp.where(s < n - 1, 1, 0)
     )
 
-    start_halo(v_ref, halo_v, 0)
     for tick in range(12 + GROUPS):
+        if tick == QUERY_TICK:
+            loads[3].wait()
+            loads[4].wait()
+        if tick == GRAD_HALO:
+            loads[2].wait()
         for g in range(GROUPS):
             step = tick - g
             if 0 <= step <= 12:
                 chain(step, g)
-        if tick == 4:
-            start_halo(g_ref, halo_g, 2)
-        if tick == 5 + GROUPS:
+        for p in range(pieces):
+            if tick == VALUE_HALO + p:
+                start_halo(v_ref, halo_v, 0, p)
+            if tick == GRAD_HALO + p:
+                start_halo(g_ref, halo_g, 2, p)
+        g = tick - FORWARD_TICK
+        if g == 0:
             wait_halo(v_ref, halo_v, 0)
-            over_lanes(finish_forward)
+        if 0 <= g < GROUPS:
+            over_lanes(finish_forward, g)
+        g = tick - CONV_TICK
+        if g == 0:
             wait_halo(g_ref, halo_g, 2)
-            over_lanes(conv_grads)
-    over_lanes(finish_backward)
+        if 0 <= g < GROUPS:
+            over_lanes(conv_grads, g)
+        g = tick - 12
+        if 0 <= g < GROUPS:
+            over_lanes(finish_backward, g)
 
     drain_halo(v_ref, halo_v, 0)
     drain_halo(g_ref, halo_g, 2)
@@ -409,18 +456,21 @@
         return pltpu.VMEM(tuple(max(1, e) for e in shape), dtype)
 
     lead = (2, GROUPS)
-    sems = [dma(4), dma(4)]
+    sems = [dma(4, cols // PIECE), dma(4, cols // PIECE)]
     for tail in ((n1 - 1,), (n2 - 1,), (), (nz - 1,), (n2 - 1,), (n1 - 1,)):
         sems += [dma(*lead, *tail), dma(*lead, *tail)]
     outs = pl.pallas_call(
         functools.partial(kernel, nz, n1, n2, chunk),
         out_shape=[jax.ShapeDtypeStruct(shape3, BF)] * 4,
-        in_specs=[vmem] * 5,
+        in_specs=[pl.BlockSpec(memory_space=pltpu.HBM)] * 5,
         out_specs=[vmem] * 4,
         scratch_shapes=[
+            buf(shape3, BF), buf(shape3, BF), buf(shape3, BF), buf(conv_weight.shape, BF),
+            buf(shape3, BF), dma(5),
             buf((HEADS, tokens, LANES), BF),
             buf((HEADS, tokens, HD), BF),
             buf((HEADS, tokens, LANES), BF),
+            buf((tokens, width), F32),
             buf((tokens, width), F32),
             buf((tokens, width), F32),
             buf((tokens, width), F32),

time: 95.6 us -> 83 us (0.87)
  Pallas kernels: 86.2 us -> 73.7 us
    pallas_call x1, Pallas kernels: 86.2 us -> 73.7 us  [on_device(): pl.pallas_call(functools.partial(kernel, nz, n1, n2, chunk), out_shape=[j...]
where the time goes in v1:
time: 83 us; the launch traced here: 82.7 us
  Pallas kernels  73.7 us (89%)
  local copies, waits for them, and re-layouts  8.32 us (10%)
    pallas_call x1, Pallas kernels, on_device(): pl.pallas_call(functools.partial(kernel, nz, n1, n2, chunk), out_shape=[j...  73.7 us
    unnamed x14, local copies, waits for them, and re-layouts  8.32 us

profile of v1, /device:TPU:0, one launch (start us, length us, event | category | flops | bytes accessed | tf_op | source)
XLA Modules:
  0.0 82.7 jit_solution(9197490850643661997)
XLA Ops:
  0.6 0.0 copy-start
  0.6 1.1 %copy-done = bf16[1,2,64,2240]{3,2,1,0:T(8,128)(2,1)S(1)} copy-done((bf16[1,2,64,2240]{3,2,1,0:T(8,128)(2,1)S(1)}, bf16[1,2,64,2240]{3,2,1,0:T(8,128)(2,1)}, u32[]{:S(2)}) %copy-start) | copy-done | bytes 573464
  1.7 0.0 copy-start.1
  1.7 1.1 %copy-done.1 = bf16[1,2,64,2240]{3,2,1,0:T(8,128)(2,1)S(1)} copy-done((bf16[1,2,64,2240]{3,2,1,0:T(8,128)(2,1)S(1)}, bf16[1,2,64,2240]{3,2,1,0:T(8,128)(2,1)}, u32[]{:S(2)}) %copy-start.1) | copy-done | bytes 573464
  2.8 0.0 copy-start.2
  2.8 1.1 %copy-done.2 = bf16[1,2,64,2240]{3,2,1,0:T(8,128)(2,1)S(1)} copy-done((bf16[1,2,64,2240]{3,2,1,0:T(8,128)(2,1)S(1)}, bf16[1,2,64,2240]{3,2,1,0:T(8,128)(2,1)}, u32[]{:S(2)}) %copy-start.2) | copy-done | bytes 573464
  3.8 0.0 copy-start.3
  3.8 1.1 %copy-done.3 = bf16[1,2,64,2240]{3,2,1,0:T(8,128)(2,1)S(1)} copy-done((bf16[1,2,64,2240]{3,2,1,0:T(8,128)(2,1)S(1)}, bf16[1,2,64,2240]{3,2,1,0:T(8,128)(2,1)}, u32[]{:S(2)}) %copy-start.3) | copy-done | bytes 573464
  4.9 0.0 copy-start.4
  4.9 0.8 copy-done.4
  5.7 73.7 %shard_map.84 = (bf16[2,64,2240]{2,1,0:T(8,128)(2,1)S(1)}, bf16[2,64,2240]{2,1,0:T(8,128)(2,1)S(1)}, bf16[2,64,2240]{2,1,0:T(8,128)(2,1)S(1)}, bf16[2,64,2240]{2,1,0:T(8,128)(2,1)S(1)}) custom-call(bf16[2,64,2240]{2,1,0:T(8,128)(2,1)S(1)} %bitcast.12, bf16[2,64,2240]{2,1,0:T(8,128)(2,1)S(1)} %bitcast.13, bf16[2,64,2240]{2,1,0:T(8,128)(2,1)S(1)} %bitcast.14, ...), custom_call_target="tpu_custom_call" | custom-call | tf_op jit(solution)/shard_map/pallas_call | solution.py:462
  79.4 0.8 copy.13
  80.2 0.8 copy.14
  81.1 0.8 copy.15
  81.9 0.8 copy.16
Async XLA Ops:
  0.6 1.1 %copy-start = (bf16[1,2,64,2240]{3,2,1,0:T(8,128)(2,1)S(1)}, bf16[1,2,64,2240]{3,2,1,0:T(8,128)(2,1)}, u32[]{:S(2)}) copy-start(bf16[1,2,64,2240]{3,2,1,0:T(8,128)(2,1)} %param.5) | copy-start | bytes 1720324
  1.7 1.1 %copy-start.1 = (bf16[1,2,64,2240]{3,2,1,0:T(8,128)(2,1)S(1)}, bf16[1,2,64,2240]{3,2,1,0:T(8,128)(2,1)}, u32[]{:S(2)}) copy-start(bf16[1,2,64,2240]{3,2,1,0:T(8,128)(2,1)} %param.6) | copy-start | bytes 1720324
  2.8 1.1 %copy-start.2 = (bf16[1,2,64,2240]{3,2,1,0:T(8,128)(2,1)S(1)}, bf16[1,2,64,2240]{3,2,1,0:T(8,128)(2,1)}, u32[]{:S(2)}) copy-start(bf16[1,2,64,2240]{3,2,1,0:T(8,128)(2,1)} %param.7) | copy-start | bytes 1720324
  3.8 1.1 %copy-start.3 = (bf16[1,2,64,2240]{3,2,1,0:T(8,128)(2,1)S(1)}, bf16[1,2,64,2240]{3,2,1,0:T(8,128)(2,1)}, u32[]{:S(2)}) copy-start(bf16[1,2,64,2240]{3,2,1,0:T(8,128)(2,1)} %param.9) | copy-start | bytes 1720324
  4.9 0.8 copy-start.4
